TPU v7x, 32 devices: a whole 2x2x4 slice. The times are simulated.
32 devices in a mesh: groups: 2 (over y), span: 4 (over z), section: 2 (over x), mp: 2 (over core).
Axes of the slice: x: 2, y: 2, z: 4, core: 2. Of those that a mesh axis runs over, the one named last changes fastest.
Arguments:
- activations: bfloat16 [2, 2560, 3072], P('section', ('groups', 'span'), 'mp'), parts along dimension 1, may hold values from -6 to 6
- projected: bfloat16 [2, 3, 2560, 3072], P('section', None, ('groups', 'span'), 'mp'), parts along dimension 2, may hold values from -6 to 6
- noise_levels: int32 [2, 8], P('section', ('groups', 'span')), parts along dimension 1, may hold values from 0 to 15
- frame_counts: int32 [2, 8], P('section', 'groups'), parts along dimension 1, may hold values from 1 to 16, as said below
- span_mask: int32 [8, 4], P('groups'), parts along dimension 0, may hold values from 0 to 1, as said below
- gates: float32 [2, 16, 3072], P('section', None, 'mp'), may hold values from -4 to 4
- norm_gains: float32 [2, 2, 24, 128], P('section', None, 'mp'), may hold values from 1.2 to 2
Outputs:
- handed: bfloat16 [2, 2560, 3072], P('section', ('groups', 'span'), 'mp'), parts along dimension 1
There are 2 independent parts, one for each index of `groups`. A program takes and returns all parts, laid end to end along the dimension named above; an argument that names none is the same for every part. Nothing has to cross between parts.
Inputs may be any that keep to these rules, and one draw needn't show every extreme that they name: `frame_counts`: some entry equals 16 and some entry equals 1. span_mask[c][c] = 1; span_mask[c][j] = 0 where j > c or j < c - 2; some row c has span_mask[c][c - 2] = 1.
All inputs are finite; a program needn't handle non-finite values.
Results may differ from a plain program's by a relative error of at most 0.0046.
Values may be sent and summed in bfloat16 or wider, within the bound.
A program may use at most 64 MiB of HBM per device.

v0:
```python
import math

import jax
import jax.numpy as jnp
from jax import lax
from jax.sharding import PartitionSpec as P

FRAMES = 16
WIN = 2


EPSILON = 1e-06


def from_behind(value, axis, by):
    devices = lax.axis_size(axis)
    pairs = [(i, i + by) for i in range(devices) if 0 <= i + by < devices]
    return lax.ppermute(value, axis, pairs)


def passed_along(value, axis, steps):
    count = lax.axis_size(axis)
    pairs = [(source, (source + steps) % count) for source in range(count)]
    return lax.ppermute(value, axis, pairs)


def normalize(values, gain_row):
    mean_square = jnp.mean(values * values, axis=-1, keepdims=True)
    return values * lax.rsqrt(mean_square + EPSILON) * gain_row


def attend_block(query_vecs, key_vecs, value_vecs, weight_row, numerator, weight_sum):
    scores = jnp.einsum(
        "qhe,khe->hqk", query_vecs, key_vecs, preferred_element_type=jnp.float32
    ) / math.sqrt(query_vecs.shape[-1])
    exp_scores = jnp.exp(scores) * weight_row[None, None, :]
    weight_sum = weight_sum + jnp.sum(exp_scores, axis=-1)
    numerator = numerator + jnp.einsum(
        "hqk,khe->qhe",
        exp_scores.astype(jnp.bfloat16),
        value_vecs,
        preferred_element_type=jnp.float32,
    )
    return (numerator, weight_sum)


def body(activations, projected, noise_levels, frame_counts, span_mask, gates, norm_gains):
    stream = activations[0].astype(jnp.float32)
    tok_count = stream.shape[0]
    feat_local = stream.shape[1]
    head_local = norm_gains.shape[2]
    head_size = norm_gains.shape[3]
    inputs = projected[0].reshape(3, tok_count, head_local, head_size)
    query_vecs = normalize(inputs[0].astype(jnp.float32), norm_gains[0, 0]).astype(jnp.bfloat16)
    key_vecs = normalize(inputs[1].astype(jnp.float32), norm_gains[0, 1]).astype(jnp.bfloat16)
    value_vecs = inputs[2]
    level_count = gates.shape[1]
    onehot = (jnp.arange(level_count, dtype=jnp.int32) == noise_levels[0, 0]).astype(jnp.float32)
    gate_row = jnp.einsum("l,lf->f", onehot, gates[0], precision=lax.Precision.HIGHEST)
    span_index = lax.axis_index("span")
    token_frame = jnp.arange(tok_count, dtype=jnp.int32) // (tok_count // FRAMES)

    def key_weight(distance):
        source = span_index - distance
        clamped = jnp.maximum(source, 0)
        allowed = (span_mask[span_index, clamped] * (source >= 0)).astype(jnp.float32)
        valid = (token_frame < frame_counts[0, clamped]).astype(jnp.float32)
        return valid * allowed

    numerator = jnp.zeros((tok_count, head_local, head_size), jnp.float32)
    weight_sum = jnp.zeros((head_local, tok_count), jnp.float32)
    numerator, weight_sum = attend_block(
        query_vecs, key_vecs, value_vecs, key_weight(0), numerator, weight_sum
    )
    payload = jnp.stack([key_vecs, value_vecs])
    passing = payload
    for distance in range(1, WIN + 1):
        passing = from_behind(passing, "span", 1)
        numerator, weight_sum = attend_block(
            query_vecs, passing[0], passing[1], key_weight(distance), numerator, weight_sum
        )
    attended = numerator / jnp.transpose(weight_sum)[:, :, None]
    gated_out = attended.reshape(tok_count, feat_local) * gate_row
    layer_out = (stream + gated_out).astype(jnp.bfloat16)
    handed = passed_along(layer_out, "section", 1)
    return handed[None]


def solution(mesh):
    placed = (
        P("section", ("groups", "span"), "mp"),
        P("section", None, ("groups", "span"), "mp"),
        P("section", ("groups", "span")),
        P("section", "groups"),
        P("groups", None),
        P("section", None, "mp"),
        P("section", None, "mp", None),
    )
    return jax.shard_map(
        body,
        mesh=mesh,
        in_specs=placed,
        out_specs=P("section", ("groups", "span"), "mp"),
        check_vma=False,
    )
```

profile of v0, /device:TPU:16, one launch (start us, length us, event | category | flops | bytes accessed | tf_op | source)
XLA Modules:
  0.0 142.6 jit_solution(11847396801299663225)
XLA Ops:
  0.0 0.0 copy-start
  0.0 0.0 copy-start.7
  0.0 4.3 %slice_convert_fusion = (f32[1,1,320,1536]{3,2,1,0:T(8,128)}, f32[1,1,320,1536]{3,2,1,0:T(8,128)}, bf16[1,1,320,1536]{3,2,1,0:T(8,128)(2,1)S(1)}) fusion(bf16[1,3,320,1536]{3,2,1,0:T(8,128)(2,1)} %param.8), kind=kLoop, calls=%fused_computation.40 | loop fusion | flops 983040 | bytes 7864320 | tf_op jit(solution)/shard_map/convert_element_type | solution.py:55
  4.4 0.0 copy-done.7
  4.4 0.7 copy.40
  5.1 0.0 copy-start.3
  5.1 0.8 copy.46
  5.9 0.3 copy-done.3
  6.2 2.0 %copy.36 = f32[1,1,320,1536]{2,3,1,0:T(8,128)S(1)} copy(f32[1,1,320,1536]{3,2,1,0:T(8,128)} %get-tuple-element.5) | data formatting | bytes 3932160 | tf_op jit(solution)/shard_map/convert_element_type | solution.py:55
  8.2 1.9 %copy.44 = f32[1,320,12,128]{3,1,2,0:T(8,128)} copy(f32[1,320,12,128]{1,3,2,0:T(8,128)S(1)} %bitcast.65) | data formatting | bytes 3932160 | tf_op jit(solution)/shard_map/convert_element_type | solution.py:55
  10.1 0.0 copy-start.5
  10.1 0.2 multiply_reduce_fusion
  10.3 1.3 copy-done.5
  11.6 0.6 multiply_convert_fusion.2
  12.2 0.0 copy-start.8
  12.2 0.0 copy-start.9
  12.2 1.5 %pad_maximum_fusion = bf16[2,320,12,128]{3,1,2,0:T(8,128)(2,1)} fusion(bf16[1,320,12,128]{3,1,2,0:T(8,128)(2,1)S(1)} %copy.46, bf16[1,320,12,128]{3,1,2,0:T(8,128)(2,1)S(1)} %multiply_convert_fusion.2), kind=kLoop, calls=%fused_computation.25 | loop fusion | flops 983040 | bytes 3932160 | tf_op jit(solution)/shard_map/stack | solution.py:75
  13.7 3.5 %collective-permute-start = (bf16[2,320,12,128]{3,1,2,0:T(8,128)(2,1)}, bf16[2,320,12,128]{3,1,2,0:T(8,128)(2,1)}, u32[]{:S(2)}, u32[]{:S(2)}) collective-permute-start(bf16[2,320,12,128]{3,1,2,0:T(8,128)(2,1)} %pad_maximum_fusion), channel_id=1, source_target_pairs={{0,4},{4,8},{8,12},{1,5},{5,9},{9,13},{2,6},{6,10},{10,14},{3,7},{... | collective-permute-start | bytes 5898248 | tf_op jit(solution)/shard_map/ppermute | solution.py:18
  17.2 0.0 copy-done.8
  17.2 0.0 copy-done.9
  17.2 0.7 constant_dynamic-slice_fusion
  18.5 3.0 %copy.34 = f32[1,1,320,1536]{2,3,1,0:T(8,128)} copy(f32[1,1,320,1536]{3,2,1,0:T(8,128)} %get-tuple-element.6) | data formatting | bytes 3932160 | tf_op jit(solution)/shard_map/convert_element_type | solution.py:54
  22.8 0.0 copy-start.1
  22.8 0.8 compare_select_fusion.1
  23.7 0.6 compare_select_fusion.2
  24.3 1.9 %multiply_reduce_fusion.1 = f32[320,12]{0,1:T(8,128)S(1)} fusion(f32[320,12,128]{0,2,1:T(8,128)} %bitcast.68), kind=kLoop, calls=%fused_computation.24 | loop fusion | flops 979200 | bytes 1981440 | tf_op jit(solution)/shard_map/reduce_sum | solution.py:28
  26.2 0.0 copy-start.6
  26.2 0.0 copy-done.1
  26.2 1.3 multiply_convert_fusion.1
  27.6 32.9 %collective-permute-done = bf16[2,320,12,128]{3,1,2,0:T(8,128)(2,1)} collective-permute-done((bf16[2,320,12,128]{3,1,2,0:T(8,128)(2,1)}, bf16[2,320,12,128]{3,1,2,0:T(8,128)(2,1)}, u32[]{:S(2)}, u32[]{:S(2)}) %collective-permute-start) | collective-permute-done | bytes 1966112 | tf_op jit(solution)/shard_map/ppermute | solution.py:18
  60.5 3.7 %collective-permute-start.1 = (bf16[2,320,12,128]{3,1,2,0:T(8,128)(2,1)}, bf16[2,320,12,128]{3,1,2,0:T(8,128)(2,1)}, u32[]{:S(2)}, u32[]{:S(2)}) collective-permute-start(bf16[2,320,12,128]{3,1,2,0:T(8,128)(2,1)} %collective-permute-done), channel_id=1, source_target_pairs={{0,4},{4,8},{8,12},{1,5},{5,9},{9,13},{2,6},{6,10},{10,14},{3,7},{... | collective-permute-start | bytes 5898248 | tf_op jit(solution)/shard_map/ppermute | solution.py:18
  64.1 0.7 compare_select_fusion
  64.8 0.0 copy-done.6
  64.8 1.4 copy.33
  66.9 0.0 copy-done
  66.9 0.2 convolution_reduce_fusion
  67.0 0.0 copy-start.4
  67.1 3.1 %fusion = (f32[12,320]{1,0:T(8,128)S(1)}, f32[12,320,320]{1,2,0:T(8,128)S(1)}) fusion(f32[320]{0:T(512)S(1)} %compare_select_fusion.2, bf16[320,12,128]{0,2,1:T(8,128)(2,1)} %multiply_convert_fusion.1, f32[320,12,128]{0,2,1:T(8,128)S(1)} %bitcast.67, f32[12,128]{1,0:T(8,128)S(1)} %bitcast.74, f32[320,12]{0,1:T(8,128)S(1)} %add_rsqrt_fusion), kind=kOutput, calls=%fused_computation.3 | convolution fusion | flops 319729920 | bytes 7902464 | tf_op jit(solution)/shard_map/qhe,khe->hqk/dot_general | solution.py:33
  70.2 0.0 copy-done.4
  70.2 0.0 copy-start.2
  70.2 1.6 %fusion.10 = f32[12,320,128]{2,1,0:T(8,128)S(1)} fusion(bf16[320,12,128]{0,2,1:T(8,128)(2,1)S(1)} %bitcast.71, f32[12,320,320]{1,2,0:T(8,128)S(1)} %get-tuple-element.19, f32[320]{0:T(512)S(1)} %compare_select_fusion.2), kind=kOutput, calls=%fused_computation.11 | convolution fusion | flops 318259200 | bytes 7865600 | tf_op jit(solution)/shard_map/hqk,khe->qhe/dot_general | solution.py:38
  71.8 0.0 copy-done.2
  71.8 2.5 %fusion.2 = (f32[12,320]{1,0:T(8,128)S(1)}, f32[12,320,320]{1,2,0:T(8,128)S(1)}) fusion(f32[320]{0:T(512)S(1)} %compare_select_fusion.1, bf16[320,12,128]{0,2,1:T(8,128)(2,1)S(1)} %copy-done.2, bf16[2,320,12,128]{3,1,2,0:T(8,128)(2,1)} %collective-permute-done), kind=kOutput, calls=%fused_computation.5 | convolution fusion | flops 318255360 | bytes 6897920 | tf_op jit(solution)/shard_map/qhe,khe->hqk/dot_general | solution.py:33
  74.3 2.7 %fusion.8 = f32[12,128,320]{1,2,0:T(8,128)S(1)} fusion(f32[12,320,320]{1,2,0:T(8,128)S(1)} %get-tuple-element.21, f32[320]{0:T(512)S(1)} %compare_select_fusion.1, bf16[2,320,12,128]{3,1,2,0:T(8,128)(2,1)} %collective-permute-done), kind=kOutput, calls=%fused_computation.10 | convolution fusion | flops 318259200 | bytes 7865600 | tf_op jit(solution)/shard_map/hqk,khe->qhe/dot_general | solution.py:38
  77.0 29.3 %collective-permute-done.1 = bf16[2,320,12,128]{3,1,2,0:T(8,128)(2,1)} collective-permute-done((bf16[2,320,12,128]{3,1,2,0:T(8,128)(2,1)}, bf16[2,320,12,128]{3,1,2,0:T(8,128)(2,1)}, u32[]{:S(2)}, u32[]{:S(2)}) %collective-permute-start.1) | collective-permute-done | bytes 1966112 | tf_op jit(solution)/shard_map/ppermute | solution.py:18
  106.4 2.5 %fusion.4 = (f32[12,320]{1,0:T(8,128)S(1)}, f32[12,320,320]{1,2,0:T(8,128)S(1)}) fusion(f32[320]{0:T(512)S(1)} %compare_select_fusion, bf16[320,12,128]{0,2,1:T(8,128)(2,1)S(1)} %copy-done.2, bf16[2,320,12,128]{3,1,2,0:T(8,128)(2,1)} %collective-permute-done.1), kind=kOutput, calls=%fused_computation.7 | convolution fusion | flops 318255360 | bytes 6897920 | tf_op jit(solution)/shard_map/qhe,khe->hqk/dot_general | solution.py:33
  108.9 4.6 %fusion.19 = f32[320,12,128]{2,0,1:T(8,128)} fusion(f32[12,128,320]{1,2,0:T(8,128)S(1)} %fusion.8, f32[12,320,128]{2,1,0:T(8,128)S(1)} %fusion.10, f32[12,320,320]{1,2,0:T(8,128)S(1)} %get-tuple-element.17, f32[320]{0:T(512)S(1)} %compare_select_fusion, bf16[2,320,12,128]{3,1,2,0:T(8,128)(2,1)} %collective-permute-done.1, f32[320,12]{0,1:T(8,128)S(1)} %add_bitcast_fusion), kind=kOutput, calls=%fused_computation.27 | convolution fusion | flops 319733760 | bytes 11813120 | tf_op jit(solution)/shard_map/hqk,khe->qhe/dot_general | solution.py:38
  113.5 2.0 %copy.51 = f32[320,12,128]{0,2,1:T(8,128)S(1)} copy(f32[320,12,128]{2,0,1:T(8,128)} %fusion.19) | data formatting | bytes 3932160 | tf_op jit(solution)/shard_map/div | solution.py:82
  115.5 2.9 %fusion.18 = bf16[320,1536]{0,1:T(8,128)(2,1)} fusion(f32[320,12,128]{0,2,1:T(8,128)S(1)} %copy.51, bf16[1,320,1536]{1,2,0:T(8,128)(2,1)} %copy.33, f32[1536]{0:T(1024)S(1)} %convolution_reduce_fusion), kind=kLoop, calls=%fused_computation.19 | loop fusion | flops 1966080 | bytes 3938304 | tf_op jit(solution)/shard_map/convert_element_type | solution.py:84
  118.4 1.5 %copy.52 = bf16[320,1536]{1,0:T(8,128)(2,1)S(1)} copy(bf16[320,1536]{0,1:T(8,128)(2,1)} %fusion.18) | data formatting | bytes 1966080 | tf_op jit(solution)/shard_map/convert_element_type | solution.py:84
  119.9 1.6 %collective-permute-start.2 = (bf16[320,1536]{1,0:T(8,128)(2,1)S(1)}, bf16[320,1536]{1,0:T(8,128)(2,1)S(1)}, u32[]{:S(2)}, u32[]{:S(2)}) collective-permute-start(bf16[320,1536]{1,0:T(8,128)(2,1)S(1)} %copy.52), channel_id=1, source_target_pairs={{0,2},{2,0},{1,3},{3,1},{4,6},{6,4},{5,7},{7,5},{8,10},{10,8},{9,1... | collective-permute-start | bytes 2949128 | tf_op jit(solution)/shard_map/ppermute | solution.py:24
  121.5 20.2 %collective-permute-done.2 = bf16[320,1536]{1,0:T(8,128)(2,1)S(1)} collective-permute-done((bf16[320,1536]{1,0:T(8,128)(2,1)S(1)}, bf16[320,1536]{1,0:T(8,128)(2,1)S(1)}, u32[]{:S(2)}, u32[]{:S(2)}) %collective-permute-start.2) | collective-permute-done | bytes 983072 | tf_op jit(solution)/shard_map/ppermute | solution.py:24
  141.7 0.9 copy.69
  (6 shorter events, 0.0 us)
Async XLA Ops:
  0.0 66.9 %copy-start = (f32[1,16,1536]{2,1,0:T(8,128)S(1)}, f32[1,16,1536]{2,1,0:T(8,128)}, u32[]{:S(2)}) copy-start(f32[1,16,1536]{2,1,0:T(8,128)} %param.12) | copy-start | bytes 294916
  0.0 4.4 %copy-start.7 = (f32[1,2,12,128]{3,1,2,0:T(2,128)S(1)}, f32[1,2,12,128]{3,1,2,0:T(2,128)}, u32[]{:S(2)}) copy-start(f32[1,2,12,128]{3,1,2,0:T(2,128)} %param.13) | copy-start | bytes 36868
  5.1 1.1 copy-start.3
  10.1 1.5 %copy-start.5 = (f32[1,320,12,128]{3,1,2,0:T(8,128)S(1)}, f32[1,320,12,128]{3,1,2,0:T(8,128)}, u32[]{:S(2)}) copy-start(f32[1,320,12,128]{3,1,2,0:T(8,128)} %copy.44) | copy-start | bytes 5898244
  12.2 5.0 %copy-start.8 = (s32[1,4]{1,0:T(1,128)S(1)}, s32[1,4]{1,0:T(1,128)}, u32[]{:S(2)}) copy-start(s32[1,4]{1,0:T(1,128)} %param.10) | copy-start | bytes 52
  12.2 5.0 %copy-start.9 = (s32[4,4]{1,0:T(4,128)S(1)}, s32[4,4]{1,0:T(4,128)}, u32[]{:S(2)}) copy-start(s32[4,4]{1,0:T(4,128)} %param.11) | copy-start | bytes 196
  13.7 46.8 %collective-permute-start = (bf16[2,320,12,128]{3,1,2,0:T(8,128)(2,1)}, bf16[2,320,12,128]{3,1,2,0:T(8,128)(2,1)}, u32[]{:S(2)}, u32[]{:S(2)}) collective-permute-start(bf16[2,320,12,128]{3,1,2,0:T(8,128)(2,1)} %pad_maximum_fusion), channel_id=1, source_target_pairs={{0,4},{4,8},{8,12},{1,5},{5,9},{9,13},{2,6},{6,10},{10,14},{3,7},{... | collective-permute-start | bytes 5898248 | tf_op jit(solution)/shard_map/ppermute | solution.py:18
  22.8 3.4 %copy-start.1 = (f32[1,1,320,1536]{2,3,1,0:T(8,128)S(1)}, f32[1,1,320,1536]{2,3,1,0:T(8,128)}, u32[]{:S(2)}) copy-start(f32[1,1,320,1536]{2,3,1,0:T(8,128)} %copy.34) | copy-start | bytes 5898244
  26.2 38.6 %copy-start.6 = (bf16[1,320,1536]{2,1,0:T(8,128)(2,1)S(1)}, bf16[1,320,1536]{2,1,0:T(8,128)(2,1)}, u32[]{:S(2)}) copy-start(bf16[1,320,1536]{2,1,0:T(8,128)(2,1)} %param.7) | copy-start | bytes 2949124
  60.5 45.9 %collective-permute-start.1 = (bf16[2,320,12,128]{3,1,2,0:T(8,128)(2,1)}, bf16[2,320,12,128]{3,1,2,0:T(8,128)(2,1)}, u32[]{:S(2)}, u32[]{:S(2)}) collective-permute-start(bf16[2,320,12,128]{3,1,2,0:T(8,128)(2,1)} %collective-permute-done), channel_id=1, source_target_pairs={{0,4},{4,8},{8,12},{1,5},{5,9},{9,13},{2,6},{6,10},{10,14},{3,7},{... | collective-permute-start | bytes 5898248 | tf_op jit(solution)/shard_map/ppermute | solution.py:18
  67.0 3.1 %copy-start.4 = (bf16[1,1,320,1536]{2,3,1,0:T(8,128)(2,1)S(1)}, bf16[1,1,320,1536]{2,3,1,0:T(8,128)(2,1)}, u32[]{:S(2)}) copy-start(bf16[1,1,320,1536]{2,3,1,0:T(8,128)(2,1)} %copy-done.3) | copy-start | bytes 2949124
  70.2 1.7 %copy-start.2 = (bf16[320,12,128]{0,2,1:T(8,128)(2,1)S(1)}, bf16[320,12,128]{0,2,1:T(8,128)(2,1)}, u32[]{:S(2)}) copy-start(bf16[320,12,128]{0,2,1:T(8,128)(2,1)} %multiply_convert_fusion.1) | copy-start | bytes 2949124
  119.9 21.8 %collective-permute-start.2 = (bf16[320,1536]{1,0:T(8,128)(2,1)S(1)}, bf16[320,1536]{1,0:T(8,128)(2,1)S(1)}, u32[]{:S(2)}, u32[]{:S(2)}) collective-permute-start(bf16[320,1536]{1,0:T(8,128)(2,1)S(1)} %copy.52), channel_id=1, source_target_pairs={{0,2},{2,0},{1,3},{3,1},{4,6},{6,4},{5,7},{7,5},{8,10},{10,8},{9,1... | collective-permute-start | bytes 2949128 | tf_op jit(solution)/shard_map/ppermute | solution.py:24
where the time goes:
time: 144 us; the launch traced here: 143 us
  waiting for transfers between devices  82.4 us (57%)
  matrix products  17.2 us (12%)
  local copies, waits for them, and re-layouts  16.6 us (12%)
  other arithmetic  14.9 us (10%)
  starting transfers between devices  8.69 us (6%)
  between operations  2.84 us (2%)
    ppermute x2, waiting for transfers between devices, from_behind(): return lax.ppermute(value, axis, pairs)  62.2 us
    ppermute x1, waiting for transfers between devices, passed_along(): return lax.ppermute(value, axis, pairs)  20.2 us
    dot_general x3, matrix products, attend_block(): jnp.einsum('hqk,khe->qhe', exp_scores.astype(jnp.bfloat16), value_vecs, p...  8.91 us
    dot_general x3, matrix products, attend_block(): jnp.einsum('qhe,khe->hqk', query_vecs, key_vecs, preferred_element_type=j...  8.13 us
    ppermute x2, starting transfers between devices, from_behind(): return lax.ppermute(value, axis, pairs)  7.13 us
    convert_element_type x1, other arithmetic, body(): inputs[1].astype(jnp.float32)  4.35 us
    unnamed x24, local copies, waits for them, and re-layouts  4.03 us
    convert_element_type x2, local copies, waits for them, and re-layouts, body(): inputs[1].astype(jnp.float32)  3.88 us
  transfers between devices with their start and end apart: 3, of which 3 were waited for; matrix products, arithmetic and copies ran while one was open for 14% of the time, Pallas kernels for 0%

commit v1 on v0

v1 whole, which is shorter than its diff:
```python
import functools
import math

import jax
import jax.numpy as jnp
from jax import lax
from jax.experimental import pallas as pl
from jax.experimental.pallas import tpu as pltpu
from jax.sharding import PartitionSpec as P

FRAMES = 16
EPSILON = 1e-06
MESH = pl.DeviceIdType.MESH
SPLIT = 2
RELAY_LAG, FAR_LAG, NEAR_LAG, OWN_LAG = 1, 2, 4, 6
MASKED = -1e30


def normalize(values, gain_row):
    values = values.astype(jnp.float32)
    mean_square = jnp.mean(values * values, axis=-1, keepdims=True)
    return (values * lax.rsqrt(mean_square + EPSILON) * gain_row).astype(jnp.bfloat16)


def kernel(
    spans, sections, steps,
    act_ref, proj_ref, noise_ref, count_ref, mask_ref, gate_ref, gain_ref,
    out_ref,
    q_own, keys, vals, q_next, q_far, far_out, far_sum, far_in, far_sum_in,
    near_out, near_sum, near_in, near_sum_in, done,
    s_own, r_own, s_rel, r_rel, s_far, r_far, s_fars, r_fars,
    s_near, r_near, s_nears, r_nears, s_out, r_out,
):
    me = lax.axis_index("span")
    section = lax.axis_index("section")
    has_prev = me > 0
    has_next = me < spans - 1
    has_far = me < spans - 2
    prev_id = {"span": jnp.maximum(me - 1, 0)}
    next_id = {"span": jnp.minimum(me + 1, spans - 1)}
    out_id = {"section": lax.rem(section + 1, sections)}
    in_id = {"section": lax.rem(section + sections - 1, sections)}

    tokens = act_ref.shape[1]
    heads = gain_ref.shape[2]
    size = gain_ref.shape[3]
    rows = tokens // SPLIT
    scale = math.log2(math.e) / math.sqrt(size)
    tiles = [(lo, min(size, rows - lo)) for lo in range(0, rows, size)]

    barrier = pltpu.get_barrier_semaphore()
    pl.semaphore_signal(barrier, inc=1, device_id=out_id, device_id_type=MESH)
    pl.semaphore_signal(barrier, inc=1, device_id=in_id, device_id_type=MESH)

    @pl.when(has_prev)
    def _():
        pl.semaphore_signal(barrier, inc=1, device_id=prev_id, device_id_type=MESH)

    @pl.when(has_next)
    def _():
        pl.semaphore_signal(barrier, inc=1, device_id=next_id, device_id_type=MESH)

    token_row = lax.broadcasted_iota(jnp.int32, (1, tokens), 1)
    valid = token_row < count_ref[0, me] * (tokens // FRAMES)

    def bias_of(distance):
        allowed = mask_ref[jnp.minimum(me + distance, spans - 1), me]
        return jnp.where(valid & (allowed > 0), 0.0, MASKED)

    eye = lax.broadcasted_iota(jnp.int32, (size, size), 0) == lax.broadcasted_iota(
        jnp.int32, (size, size), 1
    )

    def lanes(head):
        return pl.ds(pl.multiple_of(head * size, size), size)

    def prepare(head):
        keys[head] = normalize(
            proj_ref[0, 1, :, lanes(head)], gain_ref[0, 1, pl.ds(head, 1), :]
        )
        vals[head, :, :size] = proj_ref[0, 2, :, lanes(head)]
        vals[head, :, size:] = jnp.ones((tokens, size), jnp.bfloat16)
        query = normalize(
            proj_ref[0, 0, :, lanes(head)], gain_ref[0, 0, pl.ds(head, 1), :]
        )
        for part in range(SPLIT):
            q_own[head * SPLIT + part] = query[part * rows:(part + 1) * rows]

    @pl.loop(0, heads)
    def _(head):
        prepare(head)

    def attend(query, head, bias):
        scores = lax.dot_general(
            query, keys[head], (((1,), (1,)), ((), ())),
            preferred_element_type=jnp.float32,
        )
        weights = jnp.exp2(scores * scale + bias).astype(jnp.bfloat16)
        both = jnp.dot(weights, vals[head], preferred_element_type=jnp.float32)
        return both[:, :size], both[:, size:]

    def put_sum(ref, index, total):
        for n, (lo, length) in enumerate(tiles):
            picked = jnp.where(eye[:length], total[lo:lo + length], 0.0)
            ref[index, :, n * size:(n + 1) * size] = jnp.sum(picked, axis=0, keepdims=True)

    def get_sum(ref, index):
        columns = []
        for n, (lo, length) in enumerate(tiles):
            row = ref[index, :, n * size:(n + 1) * size]
            picked = jnp.where(eye[:length], row, 0.0)
            columns.append(jnp.sum(picked, axis=1, keepdims=True))
        return jnp.concatenate(columns, axis=0)

    def copy(src, dst, send, recv, index, where):
        return pltpu.make_async_remote_copy(
            src_ref=src.at[index], dst_ref=dst.at[index],
            send_sem=send.at[index], recv_sem=recv.at[index],
            device_id=where, device_id_type=MESH,
        )

    def own_copy(i):
        return copy(q_own, q_next, s_own, r_own, i, prev_id)

    def relay_copy(i):
        return copy(q_next, q_far, s_rel, r_rel, i, prev_id)

    def far_copies(i):
        return (copy(far_out, far_in, s_far, r_far, i, next_id),
                copy(far_sum, far_sum_in, s_fars, r_fars, i, next_id))

    def near_copies(i):
        return (copy(near_out, near_in, s_near, r_near, i, next_id),
                copy(near_sum, near_sum_in, s_nears, r_nears, i, next_id))

    def out_copy(i):
        head, part = i // SPLIT, i % SPLIT
        place = pl.ds(pl.multiple_of(part * rows, rows), rows)
        return pltpu.make_async_remote_copy(
            src_ref=done.at[i], dst_ref=out_ref.at[0, place, lanes(head)],
            send_sem=s_out.at[i], recv_sem=r_out.at[i],
            device_id=out_id, device_id_type=MESH,
        )

    pl.semaphore_wait(
        barrier, 2 + has_prev.astype(jnp.int32) + has_next.astype(jnp.int32)
    )

    level = noise_ref[0, 0]
    bias_own, bias_near, bias_far = bias_of(0), bias_of(1), bias_of(2)

    @pl.loop(0, steps + OWN_LAG)
    def _(step):
        @pl.when((step < steps) & has_prev)
        def _():
            own_copy(step).start()

        relay = step - RELAY_LAG

        @pl.when((relay >= 0) & (relay < steps) & has_next)
        def _():
            own_copy(relay).wait_recv()

            @pl.when(has_prev)
            def _():
                relay_copy(relay).start()

        far = step - FAR_LAG

        @pl.when((far >= 0) & (far < steps) & has_far)
        def _():
            relay_copy(far).wait_recv()
            numerator, total = attend(q_far[far], far // SPLIT, bias_far)
            far_out[far] = numerator.astype(jnp.bfloat16)
            put_sum(far_sum, far, total)
            for one in far_copies(far):
                one.start()

        near = step - NEAR_LAG

        @pl.when((near >= 0) & (near < steps) & has_next)
        def _():
            numerator, total = attend(q_next[near], near // SPLIT, bias_near)

            @pl.when(has_prev)
            def _():
                for one in far_copies(near):
                    one.wait_recv()
                near_out[near] = (
                    numerator + far_in[near].astype(jnp.float32)
                ).astype(jnp.bfloat16)
                put_sum(near_sum, near, total + get_sum(far_sum_in, near))

            @pl.when(jnp.logical_not(has_prev))
            def _():
                near_out[near] = numerator.astype(jnp.bfloat16)
                put_sum(near_sum, near, total)

            for one in near_copies(near):
                one.start()

        own = step - OWN_LAG

        @pl.when((own >= 0) & (own < steps))
        def _():
            head, part = own // SPLIT, own % SPLIT
            numerator, total = attend(q_own[own], head, bias_own)
            place = pl.ds(pl.multiple_of(part * rows, rows), rows)
            stream = act_ref[0, place, lanes(head)].astype(jnp.float32)
            levels = gate_ref[0, :, lanes(head)]
            chosen = lax.broadcasted_iota(jnp.int32, levels.shape, 0) == level
            gate = jnp.sum(jnp.where(chosen, levels, 0.0), axis=0, keepdims=True)

            def finish(numerator, total):
                done[own] = (stream + numerator / total * gate).astype(jnp.bfloat16)

            @pl.when(has_prev)
            def _():
                for one in near_copies(own):
                    one.wait_recv()
                finish(
                    numerator + near_in[own].astype(jnp.float32),
                    total + get_sum(near_sum_in, own),
                )

            @pl.when(jnp.logical_not(has_prev))
            def _():
                finish(numerator, total)

            out_copy(own).start()

    @pl.loop(0, steps)
    def _(i):
        @pl.when(has_prev)
        def _():
            own_copy(i).wait_send()

        @pl.when(has_prev & has_next)
        def _():
            relay_copy(i).wait_send()

        @pl.when(has_far)
        def _():
            for one in far_copies(i):
                one.wait_send()

        @pl.when(has_next)
        def _():
            for one in near_copies(i):
                one.wait_send()

        out_copy(i).wait()


def body(spans, sections, activations, projected, noise_levels, frame_counts, span_mask, gates,
         norm_gains):
    tokens = activations.shape[1]
    heads, size = norm_gains.shape[2], norm_gains.shape[3]
    rows = tokens // SPLIT
    steps = heads * SPLIT
    wide = -(-rows // size) * size
    vmem = pl.BlockSpec(memory_space=pltpu.VMEM)
    smem = pl.BlockSpec(memory_space=pltpu.SMEM)
    piece = pltpu.VMEM((steps, rows, size), jnp.bfloat16)
    sums = pltpu.VMEM((steps, 1, wide), jnp.float32)
    work = 4 * heads * 3 * tokens * tokens * size
    return pl.pallas_call(
        functools.partial(kernel, spans, sections, steps),
        out_shape=jax.ShapeDtypeStruct(activations.shape, jnp.bfloat16),
        in_specs=[vmem, vmem, smem, smem, smem, vmem, vmem],
        out_specs=pl.BlockSpec(memory_space=pl.ANY),
        scratch_shapes=[
            piece,
            pltpu.VMEM((heads, tokens, size), jnp.bfloat16),
            pltpu.VMEM((heads, tokens, 2 * size), jnp.bfloat16),
            piece, piece, piece, sums, piece, sums, piece, sums, piece, sums, piece,
        ] + [pltpu.SemaphoreType.DMA((steps,))] * 14,
        compiler_params=pltpu.CompilerParams(
            collective_id=0, has_side_effects=True, vmem_limit_bytes=48 * 1024 * 1024
        ),
        cost_estimate=pl.CostEstimate(
            flops=work, bytes_accessed=5 * activations.size * 2,
            transcendentals=heads * 3 * tokens * tokens,
        ),
    )(activations, projected, noise_levels, frame_counts, span_mask, gates, norm_gains)


def solution(mesh):
    placed = (
        P("section", ("groups", "span"), "mp"),
        P("section", None, ("groups", "span"), "mp"),
        P("section", ("groups", "span")),
        P("section", "groups"),
        P("groups", None),
        P("section", None, "mp"),
        P("section", None, "mp", None),
    )
    return jax.shard_map(
        functools.partial(body, mesh.shape["span"], mesh.shape["section"]),
        mesh=mesh,
        in_specs=placed,
        out_specs=P("section", ("groups", "span"), "mp"),
        check_vma=False,
    )
```

time: 144 us -> 80 us (0.56)
  waiting for transfers between devices: 82.4 us -> 0 us
  Pallas kernels: 0 us -> 72.1 us
  matrix products: 17.2 us -> 0 us
  other arithmetic: 14.9 us -> 0 us
  local copies, waits for them, and re-layouts: 16.6 us -> 6.92 us
  starting transfers between devices: 8.69 us -> 0 us
  between operations: 2.84 us -> 0.67 us
    ppermute x3 -> x0, waiting for transfers between devices: 82.4 us -> none  [the longest x2 62.2 us: from_behind(): return lax.ppermute(value, axis, pairs)]
    pallas_call x0 -> x1, Pallas kernels: none -> 72.1 us  [body(): pl.pallas_call(functools.partial(kernel, spans, sections, steps), out_sha...]
    dot_general x7 -> x0, matrix products: 17.2 us -> none  [the longest x3 8.91 us: attend_block(): jnp.einsum('hqk,khe->qhe', exp_scores.astype(jnp.bfloat16), value_vecs, p...]
    convert_element_type x4 -> x0, other arithmetic: 9.18 us -> none  [the longest x1 4.35 us: body(): inputs[1].astype(jnp.float32)]
    ppermute x3 -> x0, starting transfers between devices: 8.69 us -> none  [the longest x2 7.13 us: from_behind(): return lax.ppermute(value, axis, pairs)]
    convert_element_type x4 -> x0, local copies, waits for them, and re-layouts: 8.43 us -> none  [the longest x2 3.88 us: body(): inputs[1].astype(jnp.float32)]
    unnamed x24 -> x12, local copies, waits for them, and re-layouts: 4.03 us -> 6.92 us
    mul x3 -> x0, other arithmetic: 2.13 us -> none  [key_weight(): return valid * allowed]
  transfers between devices with their start and end apart: 3 -> 0, of which waited for: 3 -> 0; matrix products, arithmetic and copies ran while one was open for 14% -> 0% of each run, Pallas kernels for 0% -> 0%
where the time goes in v1:
time: 80 us; the launch traced here: 79.7 us
  Pallas kernels  72.1 us (90%)
  local copies, waits for them, and re-layouts  6.92 us (9%)
    pallas_call x1, Pallas kernels, body(): pl.pallas_call(functools.partial(kernel, spans, sections, steps), out_sha...  72.1 us
    unnamed x12, local copies, waits for them, and re-layouts  6.92 us

profile of v1, /device:TPU:16, one launch (start us, length us, event | category | flops | bytes accessed | tf_op | source)
XLA Modules:
  0.0 79.7 jit_solution(11082274332968327167)
XLA Ops:
  0.7 0.7 copy.8.gain_ref
  1.4 0.0 copy-start
  1.4 1.8 %copy-done = bf16[1,3,320,1536]{3,2,1,0:T(8,128)(2,1)S(1)} copy-done((bf16[1,3,320,1536]{3,2,1,0:T(8,128)(2,1)S(1)}, bf16[1,3,320,1536]{3,2,1,0:T(8,128)(2,1)}, u32[]{:S(2)}) %copy-start) | copy-done | bytes 2949144
  3.2 0.0 copy-start.1
  3.2 1.2 %copy-done.1 = bf16[1,320,1536]{2,1,0:T(8,128)(2,1)S(1)} copy-done((bf16[1,320,1536]{2,1,0:T(8,128)(2,1)S(1)}, bf16[1,320,1536]{2,1,0:T(8,128)(2,1)}, u32[]{:S(2)}) %copy-start.1) | copy-done | bytes 983064
  4.4 0.0 copy-start.2
  4.4 0.9 %copy-done.2 = f32[1,16,1536]{2,1,0:T(8,128)S(1)} copy-done((f32[1,16,1536]{2,1,0:T(8,128)S(1)}, f32[1,16,1536]{2,1,0:T(8,128)}, u32[]{:S(2)}) %copy-start.2) | copy-done | bytes 98328
  5.3 0.0 copy-start.3
  5.3 0.7 copy-done.3
  6.0 0.0 copy-start.4
  6.0 0.7 copy-done.4
  6.6 72.1 %shard_map.73 = bf16[1,320,1536]{2,1,0:T(8,128)(2,1)S(1)} custom-call(bf16[1,320,1536]{2,1,0:T(8,128)(2,1)S(1)} %copy-done.1, bf16[1,3,320,1536]{3,2,1,0:T(8,128)(2,1)S(1)} %copy-done, s32[1,1]{1,0:T(1,128)S(6)} %copy.10.noise_ref, s32[1,4]{1,0:T(1,128)S(1)} %copy-done.4, s32[4,4]{1,0:T(4,128)S(1)} %copy-done.3, f32[1,16,1536]{2,1,0:T(8,128)S(1)} %copy-done.2, ...), custom_call_target="tpu_custom_call" | custom-call | flops 1887436800 | bytes 4915200 | tf_op jit(solution)/shard_map/pallas_call | solution.py:267
  78.8 0.9 %copy.11 = bf16[1,320,1536]{2,1,0:T(8,128)(2,1)} copy(bf16[1,320,1536]{2,1,0:T(8,128)(2,1)S(1)} %shard_map.73) | data formatting | bytes 1966080
Async XLA Ops:
  1.4 1.8 %copy-start = (bf16[1,3,320,1536]{3,2,1,0:T(8,128)(2,1)S(1)}, bf16[1,3,320,1536]{3,2,1,0:T(8,128)(2,1)}, u32[]{:S(2)}) copy-start(bf16[1,3,320,1536]{3,2,1,0:T(8,128)(2,1)} %proj_ref.1) | copy-start | bytes 8847364
  3.2 1.2 %copy-start.1 = (bf16[1,320,1536]{2,1,0:T(8,128)(2,1)S(1)}, bf16[1,320,1536]{2,1,0:T(8,128)(2,1)}, u32[]{:S(2)}) copy-start(bf16[1,320,1536]{2,1,0:T(8,128)(2,1)} %act_ref.1) | copy-start | bytes 2949124
  4.4 0.9 %copy-start.2 = (f32[1,16,1536]{2,1,0:T(8,128)S(1)}, f32[1,16,1536]{2,1,0:T(8,128)}, u32[]{:S(2)}) copy-start(f32[1,16,1536]{2,1,0:T(8,128)} %gate_ref.1) | copy-start | bytes 294916
  5.3 0.7 copy-start.3
  6.0 0.7 copy-start.4

commit v2 on v1

--- a/solution.py
+++ b/solution.py
@@ -12,7 +12,7 @@
 EPSILON = 1e-06
 MESH = pl.DeviceIdType.MESH
 SPLIT = 2
-RELAY_LAG, FAR_LAG, NEAR_LAG, OWN_LAG = 1, 2, 4, 6
+RELAY_LAG, FAR_LAG, NEAR_LAG, OWN_LAG = 2, 4, 7, 10
 MASKED = -1e30
 
 
@@ -24,8 +24,10 @@
 
 def kernel(
     spans, sections, steps,
+    act_hbm, proj_hbm, noise_hbm, count_hbm, mask_hbm, gate_hbm, gain_hbm,
+    out_ref,
     act_ref, proj_ref, noise_ref, count_ref, mask_ref, gate_ref, gain_ref,
-    out_ref,
+    s_load, s_small,
     q_own, keys, vals, q_next, q_far, far_out, far_sum, far_in, far_sum_in,
     near_out, near_sum, near_in, near_sum_in, done,
     s_own, r_own, s_rel, r_rel, s_far, r_far, s_fars, r_fars,
@@ -42,7 +44,7 @@
     in_id = {"section": lax.rem(section + sections - 1, sections)}
 
     tokens = act_ref.shape[1]
-    heads = gain_ref.shape[2]
+    heads = gain_ref.shape[1]
     size = gain_ref.shape[3]
     rows = tokens // SPLIT
     scale = math.log2(math.e) / math.sqrt(size)
@@ -60,6 +62,41 @@
     def _():
         pl.semaphore_signal(barrier, inc=1, device_id=next_id, device_id_type=MESH)
 
+    def lanes(head):
+        return pl.ds(pl.multiple_of(head * size, size), size)
+
+    def load(kind, head):
+        return pltpu.make_async_copy(
+            proj_hbm.at[0, kind, :, lanes(head)],
+            proj_ref.at[kind, :, lanes(head)],
+            s_load.at[kind, head],
+        )
+
+    small = [
+        pltpu.make_async_copy(src, dst, s_small.at[n])
+        for n, (src, dst) in enumerate((
+            (gain_hbm, gain_ref), (count_hbm, count_ref), (mask_hbm, mask_ref),
+            (noise_hbm, noise_ref), (gate_hbm, gate_ref), (act_hbm, act_ref),
+        ))
+    ]
+    load(0, 0).start()
+    for one in small[:4]:
+        one.start()
+
+    @pl.loop(0, heads)
+    def _(head):
+        @pl.when(head > 0)
+        def _():
+            load(0, head).start()
+
+        load(1, head).start()
+        load(2, head).start()
+
+    for one in small[4:]:
+        one.start()
+    for one in small[:4]:
+        one.wait()
+
     token_row = lax.broadcasted_iota(jnp.int32, (1, tokens), 1)
     valid = token_row < count_ref[0, me] * (tokens // FRAMES)
 
@@ -71,24 +108,20 @@
         jnp.int32, (size, size), 1
     )
 
-    def lanes(head):
-        return pl.ds(pl.multiple_of(head * size, size), size)
-
-    def prepare(head):
-        keys[head] = normalize(
-            proj_ref[0, 1, :, lanes(head)], gain_ref[0, 1, pl.ds(head, 1), :]
-        )
-        vals[head, :, :size] = proj_ref[0, 2, :, lanes(head)]
-        vals[head, :, size:] = jnp.ones((tokens, size), jnp.bfloat16)
-        query = normalize(
-            proj_ref[0, 0, :, lanes(head)], gain_ref[0, 0, pl.ds(head, 1), :]
-        )
+    def prepare_query(head):
+        load(0, head).wait()
+        query = normalize(proj_ref[0, :, lanes(head)], gain_ref[0, head, 0:1])
         for part in range(SPLIT):
             q_own[head * SPLIT + part] = query[part * rows:(part + 1) * rows]
 
-    @pl.loop(0, heads)
-    def _(head):
-        prepare(head)
+    def prepare_keys(head):
+        load(1, head).wait()
+        load(2, head).wait()
+        keys[head] = normalize(proj_ref[1, :, lanes(head)], gain_ref[0, head, 1:2])
+        vals[head, :, :size] = proj_ref[2, :, lanes(head)]
+        vals[head, :, size:] = jnp.ones((tokens, size), jnp.bfloat16)
+
+    prepare_query(0)
 
     def attend(query, head, bias):
         scores = lax.dot_general(
@@ -147,6 +180,8 @@
     )
 
     level = noise_ref[0, 0]
+    for one in small[4:]:
+        one.wait()
     bias_own, bias_near, bias_far = bias_of(0), bias_of(1), bias_of(2)
 
     @pl.loop(0, steps + OWN_LAG)
@@ -155,6 +190,10 @@
         def _():
             own_copy(step).start()
 
+        @pl.when((step % SPLIT == SPLIT - 1) & (step < steps - 1))
+        def _():
+            prepare_query(step // SPLIT + 1)
+
         relay = step - RELAY_LAG
 
         @pl.when((relay >= 0) & (relay < steps) & has_next)
@@ -166,6 +205,10 @@
                 relay_copy(relay).start()
 
         far = step - FAR_LAG
+
+        @pl.when((far >= 0) & (far < steps) & (far % SPLIT == 0))
+        def _():
+            prepare_keys(far // SPLIT)
 
         @pl.when((far >= 0) & (far < steps) & has_far)
         def _():
@@ -229,26 +272,26 @@
 
             out_copy(own).start()
 
+            @pl.when(has_prev)
+            def _():
+                own_copy(own).wait_send()
+
+            @pl.when(has_prev & has_next)
+            def _():
+                relay_copy(own).wait_send()
+
+            @pl.when(has_far)
+            def _():
+                for one in far_copies(own):
+                    one.wait_send()
+
+            @pl.when(has_next)
+            def _():
+                for one in near_copies(own):
+                    one.wait_send()
+
     @pl.loop(0, steps)
     def _(i):
-        @pl.when(has_prev)
-        def _():
-            own_copy(i).wait_send()
-
-        @pl.when(has_prev & has_next)
-        def _():
-            relay_copy(i).wait_send()
-
-        @pl.when(has_far)
-        def _():
-            for one in far_copies(i):
-                one.wait_send()
-
-        @pl.when(has_next)
-        def _():
-            for one in near_copies(i):
-                one.wait_send()
-
         out_copy(i).wait()
 
 
@@ -259,30 +302,39 @@
     rows = tokens // SPLIT
     steps = heads * SPLIT
     wide = -(-rows // size) * size
-    vmem = pl.BlockSpec(memory_space=pltpu.VMEM)
-    smem = pl.BlockSpec(memory_space=pltpu.SMEM)
+    hbm = pl.BlockSpec(memory_space=pltpu.HBM)
+    swapped_gains = jnp.transpose(norm_gains, (0, 2, 1, 3))
     piece = pltpu.VMEM((steps, rows, size), jnp.bfloat16)
     sums = pltpu.VMEM((steps, 1, wide), jnp.float32)
     work = 4 * heads * 3 * tokens * tokens * size
     return pl.pallas_call(
         functools.partial(kernel, spans, sections, steps),
         out_shape=jax.ShapeDtypeStruct(activations.shape, jnp.bfloat16),
-        in_specs=[vmem, vmem, smem, smem, smem, vmem, vmem],
+        in_specs=[hbm] * 7,
         out_specs=pl.BlockSpec(memory_space=pl.ANY),
         scratch_shapes=[
+            pltpu.VMEM(activations.shape, jnp.bfloat16),
+            pltpu.VMEM(projected.shape[1:], jnp.bfloat16),
+            pltpu.SMEM(noise_levels.shape, jnp.int32),
+            pltpu.SMEM(frame_counts.shape, jnp.int32),
+            pltpu.SMEM(span_mask.shape, jnp.int32),
+            pltpu.VMEM(gates.shape, jnp.float32),
+            pltpu.VMEM(swapped_gains.shape, jnp.float32),
+            pltpu.SemaphoreType.DMA((3, heads)),
+            pltpu.SemaphoreType.DMA((6,)),
             piece,
             pltpu.VMEM((heads, tokens, size), jnp.bfloat16),
             pltpu.VMEM((heads, tokens, 2 * size), jnp.bfloat16),
             piece, piece, piece, sums, piece, sums, piece, sums, piece, sums, piece,
         ] + [pltpu.SemaphoreType.DMA((steps,))] * 14,
         compiler_params=pltpu.CompilerParams(
-            collective_id=0, has_side_effects=True, vmem_limit_bytes=48 * 1024 * 1024
+            collective_id=0, has_side_effects=True, vmem_limit_bytes=62 * 1024 * 1024
         ),
         cost_estimate=pl.CostEstimate(
             flops=work, bytes_accessed=5 * activations.size * 2,
             transcendentals=heads * 3 * tokens * tokens,
         ),
-    )(activations, projected, noise_levels, frame_counts, span_mask, gates, norm_gains)
+    )(activations, projected, noise_levels, frame_counts, span_mask, gates, swapped_gains)
 
 
 def solution(mesh):

time: 80 us -> 68 us (0.85)
  Pallas kernels: 72.1 us -> 64.9 us
  local copies, waits for them, and re-layouts: 6.92 us -> 2.21 us
    pallas_call x1, Pallas kernels: 72.1 us -> 64.9 us  [body(): pl.pallas_call(functools.partial(kernel, spans, sections, steps), out_sha...]
    unnamed x12 -> x1, local copies, waits for them, and re-layouts: 6.92 us -> 2.21 us
where the time goes in v2:
time: 68 us; the launch traced here: 67.8 us
  Pallas kernels  64.9 us (95%)
  local copies, waits for them, and re-layouts  2.21 us (3%)
    pallas_call x1, Pallas kernels, body(): pl.pallas_call(functools.partial(kernel, spans, sections, steps), out_sha...  64.9 us
    unnamed x1, local copies, waits for them, and re-layouts  2.21 us

profile of v2, /device:TPU:16, one launch (start us, length us, event | category | flops | bytes accessed | tf_op | source)
XLA Modules:
  0.0 67.8 jit_solution(17681825338762821550)
XLA Ops:
  0.7 64.9 %shard_map.73 = bf16[1,320,1536]{2,1,0:T(8,128)(2,1)} custom-call(bf16[1,320,1536]{2,1,0:T(8,128)(2,1)} %act_hbm.1, bf16[1,3,320,1536]{3,2,1,0:T(8,128)(2,1)} %proj_hbm.1, s32[1,1]{1,0:T(1,128)S(6)} %copy.9.noise_hbm, s32[1,4]{1,0:T(1,128)} %count_hbm.1, s32[4,4]{1,0:T(4,128)} %mask_hbm.1, f32[1,16,1536]{2,1,0:T(8,128)} %gate_hbm.1, f32[1,12,2,128]{3,2,1,0:T(2,128)} %bitcast.1), custom_call_target="tpu_custom_call" | custom-call | flops 1887436800 | bytes 4915200 | tf_op jit(solution)/shard_map/pallas_call | solution.py:310
  65.6 2.2 %copy.10 = bf16[1,320,1536]{2,1,0:T(8,128)(2,1)} copy(bf16[1,320,1536]{2,1,0:T(8,128)(2,1)} %shard_map.73) | data formatting | bytes 1966080

commit v3 on v2

--- a/solution.py
+++ b/solution.py
@@ -11,8 +11,8 @@
 FRAMES = 16
 EPSILON = 1e-06
 MESH = pl.DeviceIdType.MESH
-SPLIT = 2
-RELAY_LAG, FAR_LAG, NEAR_LAG, OWN_LAG = 2, 4, 7, 10
+SPLIT = 1
+RELAY_LAG, FAR_LAG, NEAR_LAG, OWN_LAG = 1, 2, 4, 6
 MASKED = -1e30
 
 

time: 68 us -> 67.4 us (level)
  Pallas kernels: 64.9 us -> 64.2 us
    pallas_call x1, Pallas kernels: 64.9 us -> 64.2 us  [body(): pl.pallas_call(functools.partial(kernel, spans, sections, steps), out_sha...]
where the time goes in v3:
time: 67.4 us; the launch traced here: 67 us
  Pallas kernels  64.2 us (95%)
  local copies, waits for them, and re-layouts  2.21 us (3%)
    pallas_call x1, Pallas kernels, body(): pl.pallas_call(functools.partial(kernel, spans, sections, steps), out_sha...  64.2 us
    unnamed x1, local copies, waits for them, and re-layouts  2.21 us

profile of v3, /device:TPU:16, one launch (start us, length us, event | category | flops | bytes accessed | tf_op | source)
XLA Modules:
  0.0 67.0 jit_solution(9274581417131124223)
XLA Ops:
  0.7 64.2 %shard_map.73 = bf16[1,320,1536]{2,1,0:T(8,128)(2,1)} custom-call(bf16[1,320,1536]{2,1,0:T(8,128)(2,1)} %act_hbm.1, bf16[1,3,320,1536]{3,2,1,0:T(8,128)(2,1)} %proj_hbm.1, s32[1,1]{1,0:T(1,128)S(6)} %copy.9.noise_hbm, s32[1,4]{1,0:T(1,128)} %count_hbm.1, s32[4,4]{1,0:T(4,128)} %mask_hbm.1, f32[1,16,1536]{2,1,0:T(8,128)} %gate_hbm.1, f32[1,12,2,128]{3,2,1,0:T(2,128)} %bitcast.1), custom_call_target="tpu_custom_call" | custom-call | flops 1887436800 | bytes 4915200 | tf_op jit(solution)/shard_map/pallas_call | solution.py:310
  64.8 2.2 %copy.10 = bf16[1,320,1536]{2,1,0:T(8,128)(2,1)} copy(bf16[1,320,1536]{2,1,0:T(8,128)(2,1)} %shard_map.73) | data formatting | bytes 1966080

commit v4 on v3

--- a/solution.py
+++ b/solution.py
@@ -194,54 +194,6 @@
         def _():
             prepare_query(step // SPLIT + 1)
 
-        relay = step - RELAY_LAG
-
-        @pl.when((relay >= 0) & (relay < steps) & has_next)
-        def _():
-            own_copy(relay).wait_recv()
-
-            @pl.when(has_prev)
-            def _():
-                relay_copy(relay).start()
-
-        far = step - FAR_LAG
-
-        @pl.when((far >= 0) & (far < steps) & (far % SPLIT == 0))
-        def _():
-            prepare_keys(far // SPLIT)
-
-        @pl.when((far >= 0) & (far < steps) & has_far)
-        def _():
-            relay_copy(far).wait_recv()
-            numerator, total = attend(q_far[far], far // SPLIT, bias_far)
-            far_out[far] = numerator.astype(jnp.bfloat16)
-            put_sum(far_sum, far, total)
-            for one in far_copies(far):
-                one.start()
-
-        near = step - NEAR_LAG
-
-        @pl.when((near >= 0) & (near < steps) & has_next)
-        def _():
-            numerator, total = attend(q_next[near], near // SPLIT, bias_near)
-
-            @pl.when(has_prev)
-            def _():
-                for one in far_copies(near):
-                    one.wait_recv()
-                near_out[near] = (
-                    numerator + far_in[near].astype(jnp.float32)
-                ).astype(jnp.bfloat16)
-                put_sum(near_sum, near, total + get_sum(far_sum_in, near))
-
-            @pl.when(jnp.logical_not(has_prev))
-            def _():
-                near_out[near] = numerator.astype(jnp.bfloat16)
-                put_sum(near_sum, near, total)
-
-            for one in near_copies(near):
-                one.start()
-
         own = step - OWN_LAG
 
         @pl.when((own >= 0) & (own < steps))
@@ -289,6 +241,54 @@
             def _():
                 for one in near_copies(own):
                     one.wait_send()
+
+        relay = step - RELAY_LAG
+
+        @pl.when((relay >= 0) & (relay < steps) & has_next)
+        def _():
+            own_copy(relay).wait_recv()
+
+            @pl.when(has_prev)
+            def _():
+                relay_copy(relay).start()
+
+        far = step - FAR_LAG
+
+        @pl.when((far >= 0) & (far < steps) & (far % SPLIT == 0))
+        def _():
+            prepare_keys(far // SPLIT)
+
+        @pl.when((far >= 0) & (far < steps) & has_far)
+        def _():
+            relay_copy(far).wait_recv()
+            numerator, total = attend(q_far[far], far // SPLIT, bias_far)
+            far_out[far] = numerator.astype(jnp.bfloat16)
+            put_sum(far_sum, far, total)
+            for one in far_copies(far):
+                one.start()
+
+        near = step - NEAR_LAG
+
+        @pl.when((near >= 0) & (near < steps) & has_next)
+        def _():
+            numerator, total = attend(q_next[near], near // SPLIT, bias_near)
+
+            @pl.when(has_prev)
+            def _():
+                for one in far_copies(near):
+                    one.wait_recv()
+                near_out[near] = (
+                    numerator + far_in[near].astype(jnp.float32)
+                ).astype(jnp.bfloat16)
+                put_sum(near_sum, near, total + get_sum(far_sum_in, near))
+
+            @pl.when(jnp.logical_not(has_prev))
+            def _():
+                near_out[near] = numerator.astype(jnp.bfloat16)
+                put_sum(near_sum, near, total)
+
+            for one in near_copies(near):
+                one.start()
 
     @pl.loop(0, steps)
     def _(i):

time: 67.4 us -> 69 us (1.024)
  Pallas kernels: 64.2 us -> 65.8 us
    pallas_call x1, Pallas kernels: 64.2 us -> 65.8 us  [body(): pl.pallas_call(functools.partial(kernel, spans, sections, steps), out_sha...]
where the time goes in v4:
time: 69 us; the launch traced here: 68.6 us
  Pallas kernels  65.8 us (95%)
  local copies, waits for them, and re-layouts  2.21 us (3%)
    pallas_call x1, Pallas kernels, body(): pl.pallas_call(functools.partial(kernel, spans, sections, steps), out_sha...  65.8 us
    unnamed x1, local copies, waits for them, and re-layouts  2.21 us

profile of v4, /device:TPU:16, one launch (start us, length us, event | category | flops | bytes accessed | tf_op | source)
XLA Modules:
  0.0 68.6 jit_solution(5997517314043650200)
XLA Ops:
  0.7 65.8 %shard_map.73 = bf16[1,320,1536]{2,1,0:T(8,128)(2,1)} custom-call(bf16[1,320,1536]{2,1,0:T(8,128)(2,1)} %act_hbm.1, bf16[1,3,320,1536]{3,2,1,0:T(8,128)(2,1)} %proj_hbm.1, s32[1,1]{1,0:T(1,128)S(6)} %copy.9.noise_hbm, s32[1,4]{1,0:T(1,128)} %count_hbm.1, s32[4,4]{1,0:T(4,128)} %mask_hbm.1, f32[1,16,1536]{2,1,0:T(8,128)} %gate_hbm.1, f32[1,12,2,128]{3,2,1,0:T(2,128)} %bitcast.1), custom_call_target="tpu_custom_call" | custom-call | flops 1887436800 | bytes 4915200 | tf_op jit(solution)/shard_map/pallas_call | solution.py:310
  66.4 2.2 %copy.10 = bf16[1,320,1536]{2,1,0:T(8,128)(2,1)} copy(bf16[1,320,1536]{2,1,0:T(8,128)(2,1)} %shard_map.73) | data formatting | bytes 1966080
